TPU v7x, 32 devices: a whole 2x2x4 slice. The times are simulated.
32 devices in a mesh: dp: 4 (over y, x), cent: 8 (over z, core).
Axes of the slice: x: 2, y: 2, z: 4, core: 2. Of those that a mesh axis runs over, the one named last changes fastest.
Arguments:
- points: bfloat16 [4096, 768], P('dp'), may hold values from -16 to 16
- centroids: bfloat16 [16384, 768], P(('cent', 'dp')), may hold values from -24 to 24
Outputs:
- newest: bfloat16 [16384, 768], P(('cent', 'dp'))
- previous: bfloat16 [16384, 768], P(('cent', 'dp'))
- row_potential: float32 [4096], P('dp')
- list_potential: float32 [16384], P(('cent', 'dp'))
All inputs are finite; a program needn't handle non-finite values.
Results may differ from a plain program's by a relative error of at most 0.011.
Values may be sent and summed in bfloat16 or wider, within the bound.
A program may use at most 128 MiB of HBM per device.

v0:
```python
import math

import jax
import jax.numpy as jnp
from jax import lax
from jax.sharding import PartitionSpec as P

ITERS = 3


sharpness = 4.0


def column_lse(values):
    top = lax.pmax(jnp.max(values, axis=0), "dp")
    total = lax.psum(jnp.sum(jnp.exp(values - top[None, :]), axis=0), "dp")
    return top + jnp.log(total)


def row_lse(values):
    top = lax.pmax(jnp.max(values, axis=1), "cent")
    total = lax.psum(jnp.sum(jnp.exp(values - top[:, None]), axis=1), "cent")
    return top + jnp.log(total)


def score_block(rows_data, block, factor):
    product = lax.dot_general(
        rows_data, block, (((1,), (1,)), ((), ())), preferred_element_type=jnp.float32
    )
    return factor * product


def plan_sums(logits, row_pot, col_pot, rows_data):
    plan = jnp.exp(logits + row_pot[:, None] + col_pot[None, :])
    mass = jnp.sum(plan, axis=0)
    weighted = lax.dot_general(
        plan.astype(jnp.bfloat16),
        rows_data,
        (((0,), (0,)), ((), ())),
        preferred_element_type=jnp.float32,
    )
    return (weighted, mass)


def refresh(weighted, mass, used, prior):
    fresh = (weighted + prior * used.astype(jnp.float32)) / (mass + prior)[:, None]
    return fresh.astype(jnp.bfloat16)


def shards(points, centroids):
    n_data = lax.axis_size("dp")
    n_lists = lax.axis_size("cent")
    data_index = lax.axis_index("dp")
    rows, width = points.shape
    owned = centroids.shape[0]
    total_rows = rows * n_data
    total_lists = owned * n_data * n_lists
    log_ratio = math.log(total_rows / total_lists)
    prior = 0.5 * total_rows / total_lists
    factor = sharpness / math.sqrt(width)
    history = [centroids]
    row_pot = jnp.zeros((rows,), jnp.float32)
    col_pot = jnp.zeros((owned * n_data,), jnp.float32)
    for step in range(ITERS):
        used = history[max(step - 1, 0)]
        logits = score_block(points, lax.all_gather(used, "dp", axis=0, tiled=True), factor)
        col_pot = log_ratio - column_lse(logits + row_pot[:, None])
        row_pot = -row_lse(logits + col_pot[None, :])
        weighted, mass = plan_sums(logits, row_pot, col_pot, points)
        owner_weighted, owner_mass = (
            lax.psum_scatter(weighted, "dp", scatter_dimension=0, tiled=True),
            lax.psum_scatter(mass, "dp", scatter_dimension=0, tiled=True),
        )
        history.append(refresh(owner_weighted, owner_mass, used, prior))
    own_cols = lax.dynamic_slice_in_dim(col_pot, data_index * owned, owned)
    return (history[-1], history[-2], row_pot, own_cols)


def solution(mesh):
    return jax.shard_map(
        shards,
        mesh=mesh,
        in_specs=(P("dp", None), P(("cent", "dp"), None)),
        out_specs=(P(("cent", "dp"), None), P(("cent", "dp"), None), P("dp"), P(("cent", "dp"))),
        check_vma=False,
    )
```

profile of v0, /device:TPU:0, one launch (start us, length us, event | category | flops | bytes accessed | tf_op | source)
XLA Modules:
  0.0 407.7 jit_solution(18427704023233502315)
XLA Ops:
  7.2 0.0 all-gather.3.cloned.1.call-start
  7.2 0.7 all-gather.3.cloned.1.call-update
  7.9 0.0 reduce-scatter.4.cloned.1.call-start
  8.0 48.6 %all-gather.3.cloned.1.call-done = bf16[2048,768]{1,0:T(8,128)(2,1)} async-done(((bf16[512,768]{1,0:T(8,128)(2,1)}), bf16[2048,768]{1,0:T(8,128)(2,1)}) %all-gather.3.cloned.1.call-update) | async-done | bytes 3145744 | tf_op jit(solution)/shard_map/all_gather | solution.py:66
  56.6 7.5 %fusion.20 = (f32[2048]{0:T(1024)S(1)}, f32[1024,2048]{1,0:T(8,128)}) fusion(bf16[1024,768]{1,0:T(8,128)(2,1)S(1)} %copy-done, bf16[2048,768]{1,0:T(8,128)(2,1)} %all-gather.3.cloned.1.call-done), kind=kOutput, calls=%fused_computation.45 | convolution fusion | flops 3225417728 | bytes 13115392 | tf_op jit(solution)/shard_map/dot_general | solution.py:27
  64.1 9.1 %pmax.42 = f32[2048]{0:T(1024)S(1)} all-reduce(f32[2048]{0:T(1024)S(1)} %get-tuple-element.10), channel_id=1, replica_groups=mesh['dp'=4,'cent'=8] {'dp'}, use_global_device_ids=true, to_apply=%region_1.0 | all-reduce | flops 2048 | bytes 16384 | tf_op jit(solution)/shard_map/pmax | solution.py:15
  73.2 4.5 %exponential_reduce_fusion.5 = f32[2048]{0:T(1024)S(1)} fusion(f32[1024,2048]{1,0:T(8,128)} %get-tuple-element.11, f32[2048]{0:T(1024)S(1)} %pmax.42), kind=kLoop, calls=%fused_computation.8 | loop fusion | flops 4192256 | bytes 8404992 | tf_op jit(solution)/shard_map/reduce_sum | solution.py:16
  77.7 9.0 %psum.42 = f32[2048]{0:T(1024)S(1)} all-reduce(f32[2048]{0:T(1024)S(1)} %exponential_reduce_fusion.5), channel_id=1, replica_groups=mesh['dp'=4,'cent'=8] {'dp'}, use_global_device_ids=true, to_apply=%region_3.0 | all-reduce | flops 2048 | bytes 16384 | tf_op jit(solution)/shard_map/psum | solution.py:16
  86.7 4.0 add_reduce_fusion.3
  90.7 13.6 %pmax.43 = f32[1024]{0:T(1024)S(1)} all-reduce(f32[1024]{0:T(1024)S(1)} %add_reduce_fusion.3), channel_id=1, replica_groups=mesh['dp'=4,'cent'=8] {'cent'}, use_global_device_ids=true, to_apply=%region_5.0 | all-reduce | flops 1024 | bytes 8192 | tf_op jit(solution)/shard_map/pmax | solution.py:21
  104.3 4.4 %exponential_reduce_fusion.4 = f32[1024]{0:T(1024)S(1)} fusion(f32[1024,2048]{1,0:T(8,128)} %get-tuple-element.11, f32[1024]{0:T(1024)S(1)} %pmax.43, f32[2048]{0:T(1024)S(1)} %add_subtract_fusion.2), kind=kLoop, calls=%fused_computation.7 | loop fusion | flops 6290432 | bytes 8404992 | tf_op jit(solution)/shard_map/reduce_sum | solution.py:22
  108.7 13.6 %psum.43 = f32[1024]{0:T(1024)S(1)} all-reduce(f32[1024]{0:T(1024)S(1)} %exponential_reduce_fusion.4), channel_id=1, replica_groups=mesh['dp'=4,'cent'=8] {'cent'}, use_global_device_ids=true, to_apply=%region_7.0 | all-reduce | flops 1024 | bytes 8192 | tf_op jit(solution)/shard_map/psum | solution.py:22
  122.3 9.9 %fusion.10 = f32[2048,768]{1,0:T(8,128)} fusion(bf16[1024,768]{1,0:T(8,128)(2,1)S(1)} %copy-done, f32[1024,2048]{1,0:T(8,128)} %get-tuple-element.11, f32[1024]{0:T(1024)S(1)} %add_negate_fusion.2, f32[2048]{0:T(1024)S(1)} %add_subtract_fusion.2), kind=kOutput, calls=%fused_computation.23 | convolution fusion | flops 3227516928 | bytes 16265216 | tf_op jit(solution)/shard_map/dot_general | solution.py:36
  132.3 0.0 all-gather.5.cloned.1.call-start
  132.3 0.6 dynamic-slice
  133.6 4.9 %add_reduce_fusion.4 = f32[2048]{0:T(1024)S(1)} fusion(f32[1024,2048]{1,0:T(8,128)} %get-tuple-element.11, f32[1024]{0:T(1024)S(1)} %add_negate_fusion.2), kind=kLoop, calls=%fused_computation.19 | loop fusion | flops 4192256 | bytes 8400896 | tf_op jit(solution)/shard_map/reduce_max | solution.py:15
  138.5 8.7 %pmax.44 = f32[2048]{0:T(1024)S(1)} all-reduce(f32[2048]{0:T(1024)S(1)} %add_reduce_fusion.4), channel_id=1, replica_groups=mesh['dp'=4,'cent'=8] {'dp'}, use_global_device_ids=true, to_apply=%region_12.0 | all-reduce | flops 2048 | bytes 16384 | tf_op jit(solution)/shard_map/pmax | solution.py:15
  147.2 5.3 %exponential_reduce_fusion.3 = (f32[2048]{0:T(1024)S(1)}, f32[2048]{0:T(1024)S(1)}) fusion(f32[1024,2048]{1,0:T(8,128)} %get-tuple-element.11, f32[2048]{0:T(1024)S(1)} %pmax.44, f32[1024]{0:T(1024)S(1)} %add_negate_fusion.2, f32[2048]{0:T(1024)S(1)} %add_subtract_fusion.2), kind=kLoop, calls=%fused_computation.5 | loop fusion | flops 10481664 | bytes 8425472 | tf_op jit(solution)/shard_map/reduce_sum | solution.py:16
  152.6 15.5 %all-reduce.4 = (f32[2048]{0:T(1024)S(1)}, f32[2048]{0:T(1024)S(1)}) all-reduce(f32[2048]{0:T(1024)S(1)} %get-tuple-element.5, f32[2048]{0:T(1024)S(1)} %get-tuple-element.4), channel_id=3, replica_groups=mesh['dp'=4,'cent'=8] {'dp'}, use_global_device_ids=true, to_apply=%region_10.0.clone | all-reduce | flops 4096 | bytes 32768
  168.0 0.1 dynamic-slice_add_fusion.2
  168.1 32.7 %reduce-scatter.4.cloned.1.call-done = f32[512,768]{1,0:T(8,128)} async-done(((f32[2048,768]{1,0:T(8,128)}), f32[512,768]{1,0:T(8,128)}) %reduce-scatter.4.cloned.1.call-update) | async-done | bytes 1572880 | tf_op jit(solution)/shard_map/reduce_scatter | solution.py:71
  200.8 2.5 divide_convert_fusion.2
  203.3 0.0 all-gather.5.cloned.1.call-update
  203.3 0.2 reduce-scatter.8.cloned.1.call-start
  203.6 4.0 add_reduce_fusion.2
  207.6 16.4 %pmax.45 = f32[1024]{0:T(1024)S(1)} all-reduce(f32[1024]{0:T(1024)S(1)} %add_reduce_fusion.2), channel_id=1, replica_groups=mesh['dp'=4,'cent'=8] {'cent'}, use_global_device_ids=true, to_apply=%region_16.0 | all-reduce | flops 1024 | bytes 8192 | tf_op jit(solution)/shard_map/pmax | solution.py:21
  224.0 4.4 %exponential_reduce_fusion.2 = f32[1024]{0:T(1024)S(1)} fusion(f32[1024,2048]{1,0:T(8,128)} %get-tuple-element.11, f32[1024]{0:T(1024)S(1)} %pmax.45, f32[2048]{0:T(1024)S(1)} %add_subtract_fusion.1), kind=kLoop, calls=%fused_computation.4 | loop fusion | flops 6290432 | bytes 8404992 | tf_op jit(solution)/shard_map/reduce_sum | solution.py:22
  228.4 13.6 %psum.45 = f32[1024]{0:T(1024)S(1)} all-reduce(f32[1024]{0:T(1024)S(1)} %exponential_reduce_fusion.2), channel_id=1, replica_groups=mesh['dp'=4,'cent'=8] {'cent'}, use_global_device_ids=true, to_apply=%region_18.0 | all-reduce | flops 1024 | bytes 8192 | tf_op jit(solution)/shard_map/psum | solution.py:22
  242.0 9.9 %fusion.6 = f32[2048,768]{1,0:T(8,128)} fusion(bf16[1024,768]{1,0:T(8,128)(2,1)S(1)} %copy-done, f32[1024,2048]{1,0:T(8,128)} %get-tuple-element.11, f32[1024]{0:T(1024)S(1)} %add_negate_fusion.1, f32[2048]{0:T(1024)S(1)} %add_subtract_fusion.1), kind=kOutput, calls=%fused_computation.21 | convolution fusion | flops 3227516928 | bytes 16265216 | tf_op jit(solution)/shard_map/dot_general | solution.py:36
  251.9 0.0 reduce-scatter.6.cloned.1.call-start
  251.9 0.0 all-gather.5.cloned.1.call-done
  252.0 7.6 %add_reduce_fusion.1 = (f32[2048]{0:T(1024)S(1)}, f32[2048,1024]{0,1:T(8,128)}) fusion(f32[1024]{0:T(1024)S(1)} %add_negate_fusion.1, bf16[2048,768]{1,0:T(8,128)(2,1)} %all-gather.5.cloned.1.call-done, bf16[1024,768]{1,0:T(8,128)(2,1)S(1)} %copy-done), kind=kOutput, calls=%fused_computation.10 | convolution fusion | flops 3227514880 | bytes 13119488 | tf_op jit(solution)/shard_map/dot_general | solution.py:27
  259.5 9.6 %pmax.46 = f32[2048]{0:T(1024)S(1)} all-reduce(f32[2048]{0:T(1024)S(1)} %get-tuple-element.12), channel_id=1, replica_groups=mesh['dp'=4,'cent'=8] {'dp'}, use_global_device_ids=true, to_apply=%region_20.0 | all-reduce | flops 2048 | bytes 16384 | tf_op jit(solution)/shard_map/pmax | solution.py:15
  269.1 4.7 %exponential_reduce_fusion.1 = f32[2048]{0:T(1024)S(1)} fusion(f32[2048,1024]{0,1:T(8,128)} %get-tuple-element.13, f32[2048]{0:T(1024)S(1)} %pmax.46, f32[1024]{0:T(1024)S(1)} %add_negate_fusion.1), kind=kLoop, calls=%fused_computation.3 | loop fusion | flops 8386560 | bytes 8409088 | tf_op jit(solution)/shard_map/reduce_sum | solution.py:16
  273.9 9.3 %psum.46 = f32[2048]{0:T(1024)S(1)} all-reduce(f32[2048]{0:T(1024)S(1)} %exponential_reduce_fusion.1), channel_id=1, replica_groups=mesh['dp'=4,'cent'=8] {'dp'}, use_global_device_ids=true, to_apply=%region_22.0 | all-reduce | flops 2048 | bytes 16384 | tf_op jit(solution)/shard_map/psum | solution.py:16
  283.2 4.3 %add_reduce_fusion = f32[1024]{0:T(1024)S(1)} fusion(f32[2048,1024]{0,1:T(8,128)} %get-tuple-element.13, f32[2048]{0:T(1024)S(1)} %add_subtract_fusion), kind=kLoop, calls=%fused_computation.9 | loop fusion | flops 6290432 | bytes 8400896 | tf_op jit(solution)/shard_map/reduce_max | solution.py:21
  287.5 13.6 %pmax.47 = f32[1024]{0:T(1024)S(1)} all-reduce(f32[1024]{0:T(1024)S(1)} %add_reduce_fusion), channel_id=1, replica_groups=mesh['dp'=4,'cent'=8] {'cent'}, use_global_device_ids=true, to_apply=%region_24.0 | all-reduce | flops 1024 | bytes 8192 | tf_op jit(solution)/shard_map/pmax | solution.py:21
  301.1 4.6 %exponential_reduce_fusion = f32[1024]{0:T(1024)S(1)} fusion(f32[2048,1024]{0,1:T(8,128)} %get-tuple-element.13, f32[1024]{0:T(1024)S(1)} %pmax.47, f32[2048]{0:T(1024)S(1)} %add_subtract_fusion), kind=kLoop, calls=%fused_computation.2 | loop fusion | flops 8387584 | bytes 8404992 | tf_op jit(solution)/shard_map/reduce_sum | solution.py:22
  305.6 13.9 %psum.47 = f32[1024]{0:T(1024)S(1)} all-reduce(f32[1024]{0:T(1024)S(1)} %exponential_reduce_fusion), channel_id=1, replica_groups=mesh['dp'=4,'cent'=8] {'cent'}, use_global_device_ids=true, to_apply=%region_26.0 | all-reduce | flops 1024 | bytes 8192 | tf_op jit(solution)/shard_map/psum | solution.py:22
  319.6 10.3 %fusion.8 = f32[2048,768]{1,0:T(8,128)} fusion(bf16[1024,768]{1,0:T(8,128)(2,1)S(1)} %copy-done, f32[2048,1024]{0,1:T(8,128)} %get-tuple-element.13, f32[1024]{0:T(1024)S(1)} %add_negate_fusion, f32[2048]{0:T(1024)S(1)} %add_subtract_fusion), kind=kOutput, calls=%fused_computation.22 | convolution fusion | flops 3229614080 | bytes 16265216 | tf_op jit(solution)/shard_map/dot_general | solution.py:36
  330.0 4.4 %fusion.4 = f32[2048]{0:T(1024)S(1)} fusion(f32[1024,2048]{1,0:T(8,128)} %get-tuple-element.11, f32[1024]{0:T(1024)S(1)} %add_negate_fusion.1, f32[2048]{0:T(1024)S(1)} %add_subtract_fusion.1), kind=kLoop, calls=%fused_computation.17 | loop fusion | flops 6289408 | bytes 8409088 | tf_op jit(solution)/shard_map/reduce_sum | solution.py:35
  334.4 0.7 dynamic_slice.3
  335.0 4.6 %fusion.2 = f32[2048]{0:T(1024)S(1)} fusion(f32[2048,1024]{0,1:T(8,128)} %get-tuple-element.13, f32[1024]{0:T(1024)S(1)} %add_negate_fusion, f32[2048]{0:T(1024)S(1)} %add_subtract_fusion), kind=kLoop, calls=%fused_computation.15 | loop fusion | flops 8386560 | bytes 8409088 | tf_op jit(solution)/shard_map/reduce_sum | solution.py:35
  339.6 16.6 %all-reduce.3 = (f32[2048]{0:T(1024)S(1)}, f32[2048]{0:T(1024)S(1)}) all-reduce(f32[2048]{0:T(1024)S(1)} %fusion.2, f32[2048]{0:T(1024)S(1)} %fusion.4), channel_id=5, replica_groups=mesh['dp'=4,'cent'=8] {'dp'}, use_global_device_ids=true, to_apply=%region_29.0.clone | all-reduce | flops 4096 | bytes 32768
  356.2 0.1 dynamic-slice_add_fusion
  356.3 2.5 divide_convert_fusion
  358.8 39.8 %reduce-scatter.6.cloned.1.call-done = f32[512,768]{1,0:T(8,128)} async-done(((f32[2048,768]{1,0:T(8,128)}), f32[512,768]{1,0:T(8,128)}) %reduce-scatter.6.cloned.1.call-update) | async-done | bytes 1572880 | tf_op jit(solution)/shard_map/reduce_scatter | solution.py:71
  398.6 2.5 divide_convert_fusion.1
  (20 shorter events, 0.1 us)
Async XLA Ops:
  7.2 49.4 %copy-start = (bf16[1024,768]{1,0:T(8,128)(2,1)S(1)}, bf16[1024,768]{1,0:T(8,128)(2,1)}, u32[]{:S(2)}) copy-start(bf16[1024,768]{1,0:T(8,128)(2,1)} %param.2) | copy-start | bytes 4718596
  7.2 49.4 %all-gather.3.cloned.1.call-start = ((), (), s32[]{:S(2)}) async-start(), calls=%async_computation.3 | async-start | bytes 3932160 | tf_op jit(solution)/shard_map/all_gather | solution.py:66
  7.9 192.9 %reduce-scatter.4.cloned.1.call-start = ((), (), s32[]{:S(2)}) async-start(), calls=%async_computation.4 | async-start | bytes 7864320 | tf_op jit(solution)/shard_map/reduce_scatter | solution.py:71
  122.3 10.0 %copy-start.4 = (u32[32]{0:T(128)S(1)}, u32[32]{0:T(128)}, u32[]{:S(2)}) copy-start(u32[32]{0:T(128)} %constant.24) | copy-start | bytes 388
  132.3 119.7 %all-gather.5.cloned.1.call-start = ((), (), s32[]{:S(2)}) async-start(), calls=%async_computation.5 | async-start | bytes 3932160 | tf_op jit(solution)/shard_map/all_gather | solution.py:66
  133.6 67.2 %copy-start.1 = (bf16[512,768]{1,0:T(8,128)(2,1)S(1)}, bf16[512,768]{1,0:T(8,128)(2,1)}, u32[]{:S(2)}) copy-start(bf16[512,768]{1,0:T(8,128)(2,1)} %param.3) | copy-start | bytes 2359300
  203.3 152.9 %reduce-scatter.8.cloned.1.call-start = ((), (), s32[]{:S(2)}) async-start(), calls=%async_computation.7 | async-start | bytes 7864320 | tf_op jit(solution)/shard_map/reduce_scatter | solution.py:71
  251.9 146.7 %reduce-scatter.6.cloned.1.call-start = ((), (), s32[]{:S(2)}) async-start(), calls=%async_computation.6 | async-start | bytes 7864320 | tf_op jit(solution)/shard_map/reduce_scatter | solution.py:71
  319.6 15.4 %copy-start.3 = (f32[1024]{0:T(1024)}, f32[1024]{0:T(1024)S(1)}, u32[]{:S(2)}) copy-start(f32[1024]{0:T(1024)S(1)} %add_negate_fusion) | copy-start | bytes 12292
  330.0 68.6 %copy-start.2 = (bf16[512,768]{1,0:T(8,128)(2,1)S(1)}, bf16[512,768]{1,0:T(8,128)(2,1)}, u32[]{:S(2)}) copy-start(bf16[512,768]{1,0:T(8,128)(2,1)} %divide_convert_fusion.2) | copy-start | bytes 2359300
Sparse Core Ops, SparseCore 0:
  9.9 46.6 all-gather.2
  132.4 68.3 reduce-scatter.3
  203.5 43.9 all-gather.4
  252.0 69.3 reduce-scatter.7
  330.1 68.4 reduce-scatter.5
where the time goes:
time: 408 us
  blocking collectives  162 us (40%)
  waiting for transfers between devices  122 us (30%)
  other arithmetic  61.8 us (15%)
  matrix products  45.3 us (11%)
  between operations  14.6 us (4%)
    reduce_scatter x3, waiting for transfers between devices, shards(): lax.psum_scatter(weighted, 'dp', scatter_dimension=0, tiled=True)  72.4 us
    all_gather x2, waiting for transfers between devices, shards(): lax.all_gather(used, 'dp', axis=0, tiled=True)  48.6 us
    pmax x3, blocking collectives, row_lse(): top = lax.pmax(jnp.max(values, axis=1), 'cent')  43.6 us
    psum x3, blocking collectives, row_lse(): total = lax.psum(jnp.sum(jnp.exp(values - top[:, None]), axis=1), 'cent')  41.1 us
    unnamed x2, blocking collectives  32.1 us
    dot_general x3, matrix products, plan_sums(): lax.dot_general(plan.astype(jnp.bfloat16), rows_data, (((0,), (0,)), ((),...  30.2 us
    pmax x3, blocking collectives, column_lse(): top = lax.pmax(jnp.max(values, axis=0), 'dp')  27.4 us
    psum x2, blocking collectives, column_lse(): total = lax.psum(jnp.sum(jnp.exp(values - top[None, :]), axis=0), 'dp')  18.3 us
  transfers between devices with their start and end apart: 5, of which 3 were waited for; matrix products, arithmetic and copies ran while one was open for 18% of the time, Pallas kernels for 0%

commit v1 on v0

v1 whole, which is shorter than its diff:
```python
import functools
import math

import jax
import jax.numpy as jnp
from jax import lax
from jax.experimental import pallas as pl
from jax.experimental.pallas import tpu as pltpu
from jax.sharding import PartitionSpec as P

sharpness = 4.0
LANES = 128
LOG2E = math.log2(math.e)
LN2 = math.log(2.0)


def flip(i, bit):
    return i + bit - 2 * bit * ((i // bit) % 2)


def tile_lanes(col, width):
    return jnp.concatenate([col] * (width // LANES), axis=1)


def lane_groups(x):
    return [x[:, g : g + LANES] for g in range(0, x.shape[1], LANES)]


def fold(op, parts):
    return functools.reduce(op, parts)


def sub8(op, x):
    return fold(op, [x[g : g + 8] for g in range(0, x.shape[0], 8)])


def kernel(
    n_dp, n_cent,
    pts_in, cen,
    newest, previous, row_out, list_out,
    pts, lt, lt2, pb, acc, c1, top, tot, cp, ratio_j, mass, row_a, row_b, row_m,
    mine, gathered, full,
    own_sem, ag_send, ag_recv, sib_send, sib_recv, x1_send, x1_recv, x2_send, x2_recv,
):
    n = n_dp * n_cent
    _, blk, width = pts_in.shape
    nb = 2 * n_dp
    lists = cen.shape[0]
    rows_all = nb * blk
    w_all = rows_all // LANES
    per = blk // LANES
    quarter = blk // 2
    log_ratio = math.log2(rows_all / (lists * n))
    prior = 0.5 * rows_all / (lists * n)
    factor = sharpness / math.sqrt(width) * LOG2E
    strip = 64
    strips = [pl.ds(s, strip) for s in range(0, lists, strip)]

    d = lax.axis_index("dp")
    k = lax.axis_index("cent")
    core = lax.rem(k, 2)
    sib = flip(k, 1)
    me = k * n_dp + d
    my_w = lax.rem(me, w_all)

    def dev(e):
        return {"dp": lax.rem(e, n_dp), "cent": e // n_dp}

    barrier = pltpu.get_barrier_semaphore()

    def greet(o, _):
        e = lax.rem(me + o, n)
        pl.semaphore_signal(barrier, inc=1, device_id=dev(e), device_id_type=pl.DeviceIdType.MESH)
        return 0

    lax.fori_loop(1, n, greet, 0)
    own_copy = pltpu.make_async_copy(pts_in, pts.at[pl.ds(2 * d, 2)], own_sem)
    own_copy.start()
    top[...] = jnp.full_like(top, -jnp.inf)
    tot[...] = jnp.zeros_like(tot)
    pl.semaphore_wait(barrier, n - 1)

    def remote(src, dst, ss, rs, to):
        return pltpu.make_async_remote_copy(
            src_ref=src, dst_ref=dst, send_sem=ss, recv_sem=rs,
            device_id=to, device_id_type=pl.DeviceIdType.MESH,
        )

    def online(x, s):
        groups = lane_groups(x)
        old = top[s, :]
        new = jnp.maximum(old, fold(jnp.maximum, groups))
        tot[s, :] = tot[s, :] * jnp.exp2(old - new) + fold(
            jnp.add, [jnp.exp2(g - new) for g in groups]
        )
        top[s, :] = new

    def dot_scores(c_ref, i, out):
        for q in range(2):
            lanes = pl.ds(q * quarter, quarter)
            out[i, :, lanes] = factor * lax.dot_general(
                c_ref[...], pts[i, lanes, :], (((1,), (1,)), ((), ())),
                preferred_element_type=jnp.float32,
            )

    def first_scores(i):
        dot_scores(cen, i, lt)
        for s in strips:
            online(lt[i, s, :], s)

    def many_scores(blocks):
        def body(t, _):
            i = blocks[0]
            for u in range(1, len(blocks)):
                i = jnp.where(t == u, blocks[u], i)
            first_scores(i)
            return 0

        lax.fori_loop(0, len(blocks), body, 0)

    def forward(slot, j, rows):
        ref = pts.at[j, rows]
        cp_ = remote(ref, ref, sib_send.at[slot], sib_recv.at[slot], {"dp": d, "cent": sib})
        cp_.start()
        return cp_

    pending = []
    if n_dp == 4:
        dx, dy = flip(d, 1), flip(d, 2)
        dd = flip(dx, 2)
        part = (pl.ds(0, quarter), pl.ds(quarter, quarter))
        hx, hy, hd, ho = 2 * dx + core, 2 * dy + core, 2 * dd + core, 2 * d + core
        to_x, to_y = {"dp": dx, "cent": k}, {"dp": dy, "cent": k}

        def own_send(slot, p, to):
            c = remote(pts_in.at[core, part[p]], pts.at[ho, part[p]], ag_send.at[slot], ag_recv.at[slot], to)
            c.start()
            return c

        def relay(slot, j, p, to):
            ref = pts.at[j, part[p]]
            c = remote(ref, ref, ag_send.at[slot], ag_recv.at[slot], to)
            c.start()
            return c

        s0 = own_send(0, 1, to_x)
        s3 = own_send(3, 0, to_y)
        s1 = own_send(1, 0, to_x)
        s4 = own_send(4, 1, to_y)
        own_copy.wait()
        many_scores([2 * d, 2 * d + 1])
        s3.wait_recv()
        s2 = relay(2, hy, 0, to_x)
        f0 = forward(0, hy, part[0])
        s0.wait_recv()
        s5 = relay(5, hx, 1, to_y)
        f1 = forward(1, hx, part[1])
        s1.wait_recv()
        f2 = forward(2, hx, part[0])
        s4.wait_recv()
        f3 = forward(3, hy, part[1])
        many_scores([hx, hy])
        for f in (f0, f1, f2, f3):
            f.wait_recv()
        many_scores([flip(hx, 1), flip(hy, 1)])
        s2.wait_recv()
        f4 = forward(4, hd, part[0])
        s5.wait_recv()
        f5 = forward(5, hd, part[1])
        many_scores([hd])
        f4.wait_recv()
        f5.wait_recv()
        many_scores([flip(hd, 1)])
        pending = [s0, s1, s2, s3, s4, s5, f0, f1, f2, f3, f4, f5]
    else:
        sends = []
        for o in range(1, n_dp):
            c = remote(
                pts_in.at[core], pts.at[2 * d + core], ag_send.at[o - 1], ag_recv.at[o - 1],
                {"dp": lax.rem(d + o, n_dp), "cent": k},
            )
            c.start()
            sends.append(c)
        own_copy.wait()
        many_scores([2 * d, 2 * d + 1])
        forwards = []
        for o in range(1, n_dp):
            sends[o - 1].wait_recv()
            j = 2 * lax.rem(d + n_dp - o, n_dp) + core
            forwards.append(forward(o - 1, j, pl.ds(0, blk)))
        for o in range(1, n_dp):
            j = 2 * lax.rem(d + n_dp - o, n_dp) + core
            many_scores([j])
            forwards[o - 1].wait_recv()
            many_scores([flip(j, 1)])
        pending = sends + forwards
    for c in pending:
        c.wait_send()

    def finish_columns():
        for s in strips:
            t = top[s, :]
            m = jnp.max(t, axis=1, keepdims=True)
            total = jnp.sum(tot[s, :] * jnp.exp2(t - m), axis=1, keepdims=True)
            cp[s, :] = jnp.broadcast_to(log_ratio - (m + jnp.log2(total)), (strip, LANES))

    def put_chunks(x, i, v):
        for g in range(per):
            mine[x, i * per + g] = v[:, g * LANES : (g + 1) * LANES]

    def row_pass(ref, x):
        def body(i, _):
            def inner(s):
                return ref[i, s, :] + tile_lanes(cp[s, :], blk)

            m8 = fold(jnp.maximum, [sub8(jnp.maximum, inner(s)) for s in strips])
            rmax = jnp.max(m8, axis=0, keepdims=True)
            part_sum = None
            for s in strips:
                e = jnp.exp2(inner(s) - rmax)
                ref[i, s, :] = e
                t = sub8(jnp.add, e)
                part_sum = t if part_sum is None else part_sum + t
            total = jnp.sum(part_sum, axis=0, keepdims=True)
            row_m[i] = rmax
            put_chunks(x, i, rmax + jnp.log2(total))
            return 0

        lax.fori_loop(0, nb, body, 0)

    def start_exchange(x):
        def send(o, _):
            e = lax.rem(me + o, n)
            remote(
                mine.at[x, lax.rem(e, w_all)], gathered.at[x, me], x1_send.at[x], x1_recv.at[x], dev(e)
            ).start()
            return 0

        lax.fori_loop(1, n, send, 0)
        gathered[x, me] = mine[x, my_w]

    def wait_bytes(ref, sem):
        pltpu.make_async_copy(ref, ref, sem).wait()

    def middle_exchange(x, logs):
        wait_bytes(gathered.at[x, pl.ds(0, n - 1)], x1_recv.at[x])
        wait_bytes(gathered.at[x, pl.ds(0, n - 1)], x1_send.at[x])
        v = gathered[x]
        if logs:
            m = jnp.max(v, axis=0, keepdims=True)
            res = m + jnp.log2(jnp.sum(jnp.exp2(v - m), axis=0, keepdims=True))
        else:
            res = jnp.sum(v, axis=0, keepdims=True)
        full[x, my_w] = res[0]

        def send(o, _):
            e = (me // w_all) * w_all + lax.rem(my_w + o, w_all)
            ref = full.at[x, my_w]
            remote(ref, ref, x2_send.at[x], x2_recv.at[x], dev(e)).start()
            return 0

        lax.fori_loop(1, w_all, send, 0)

    def end_exchange(x):
        wait_bytes(full.at[x, pl.ds(0, w_all - 1)], x2_recv.at[x])
        wait_bytes(full.at[x, pl.ds(0, w_all - 1)], x2_send.at[x])

    def full_row(x, i):
        return jnp.concatenate([full[x, i * per + g] for g in range(per)], axis=1)

    def weigh(ref, scale_of):
        mass[...] = jnp.zeros_like(mass)
        acc[...] = jnp.zeros_like(acc)

        def body(i, _):
            scale = scale_of(i)
            for s in strips:
                p = ref[i, s, :] * scale
                mass[s, :] += fold(jnp.add, lane_groups(p))
                pb[s, :] = p.astype(jnp.bfloat16)
            acc[...] += jnp.dot(pb[...], pts[i], preferred_element_type=jnp.float32)
            return 0

        lax.fori_loop(0, nb, body, 0)

    def refresh(out, used, gain):
        for s in strips:
            m = jnp.sum(mass[s, :], axis=1, keepdims=True)
            wgt = acc[s, :]
            if gain:
                r = ratio_j[s, :][:, 0:1]
                m, wgt = m * r, wgt * r
            fresh = (wgt + prior * used[s, :].astype(jnp.float32)) / (m + prior)
            out[s, :] = fresh.astype(jnp.bfloat16)

    finish_columns()
    row_pass(lt, 0)
    start_exchange(0)
    middle_exchange(0, True)
    end_exchange(0)

    def scale_0(i):
        v = jnp.exp2(row_m[i] - full_row(0, i))
        row_a[i] = v
        return v

    weigh(lt, scale_0)
    refresh(c1, cen, False)
    for s in strips:
        m = jnp.sum(mass[s, :], axis=1, keepdims=True)
        ratio_j[s, :] = jnp.broadcast_to(2.0**log_ratio / m, (strip, LANES))

    def row_sums(i, _):
        part_sum = fold(
            jnp.add,
            [sub8(jnp.add, lt[i, s, :] * tile_lanes(ratio_j[s, :], blk)) for s in strips],
        )
        put_chunks(1, i, jnp.sum(part_sum, axis=0, keepdims=True) * row_a[i])
        return 0

    lax.fori_loop(0, nb, row_sums, 0)
    start_exchange(1)

    def second_scores(i, _):
        dot_scores(c1, i, lt2)
        return 0

    lax.fori_loop(0, nb // 2, second_scores, 0)
    middle_exchange(1, False)
    lax.fori_loop(nb // 2, nb, second_scores, 0)
    end_exchange(1)

    top[...] = jnp.full_like(top, -jnp.inf)
    tot[...] = jnp.zeros_like(tot)

    def second_columns(i, _):
        t = full_row(1, i)
        row_b[i] = row_a[i] / t
        pot = -full_row(0, i) - jnp.log2(t)
        for s in strips:
            online(lt2[i, s, :] + pot, s)
        return 0

    lax.fori_loop(0, nb, second_columns, 0)
    finish_columns()
    row_pass(lt2, 2)
    start_exchange(2)
    middle_exchange(2, True)
    weigh(lt, lambda i: row_b[i])
    refresh(previous, cen, True)
    end_exchange(2)
    weigh(lt2, lambda i: jnp.exp2(row_m[i] - full_row(2, i)))
    refresh(newest, c1, False)
    for h in range(2):
        row_out[h] = -LN2 * full_row(2, 2 * d + h)
    list_out[...] = LN2 * cp[...].T[0:1, :]


def shards(n_dp, n_cent, points, centroids):
    rows, width = points.shape
    lists = centroids.shape[0]
    n = n_dp * n_cent
    blk = rows // 2
    nb = 2 * n_dp
    w_all = rows * n_dp // LANES
    f32, bf16 = jnp.float32, jnp.bfloat16
    dma = pltpu.SemaphoreType.DMA
    vmem = pl.BlockSpec(memory_space=pltpu.VMEM)
    newest, previous, row_pot, list_pot = pl.pallas_call(
        functools.partial(kernel, n_dp, n_cent),
        out_shape=(
            jax.ShapeDtypeStruct((lists, width), bf16),
            jax.ShapeDtypeStruct((lists, width), bf16),
            jax.ShapeDtypeStruct((2, 1, blk), f32),
            jax.ShapeDtypeStruct((1, lists), f32),
        ),
        in_specs=[pl.BlockSpec(memory_space=pl.ANY), vmem],
        out_specs=(vmem, vmem, vmem, vmem),
        scratch_shapes=[
            pltpu.VMEM((nb, blk, width), bf16),
            pltpu.VMEM((nb, lists, blk), f32),
            pltpu.VMEM((nb, lists, blk), f32),
            pltpu.VMEM((lists, blk), bf16),
            pltpu.VMEM((lists, width), f32),
            pltpu.VMEM((lists, width), bf16),
            pltpu.VMEM((lists, LANES), f32),
            pltpu.VMEM((lists, LANES), f32),
            pltpu.VMEM((lists, LANES), f32),
            pltpu.VMEM((lists, LANES), f32),
            pltpu.VMEM((lists, LANES), f32),
            pltpu.VMEM((nb, 1, blk), f32),
            pltpu.VMEM((nb, 1, blk), f32),
            pltpu.VMEM((nb, 1, blk), f32),
            pltpu.VMEM((3, w_all, 1, LANES), f32),
            pltpu.VMEM((3, n, 1, LANES), f32),
            pltpu.VMEM((3, w_all, 1, LANES), f32),
            dma, dma((2 * n_dp,)), dma((2 * n_dp,)), dma((2 * n_dp,)), dma((2 * n_dp,)),
            dma((3,)), dma((3,)), dma((3,)), dma((3,)),
        ],
        compiler_params=pltpu.CompilerParams(
            collective_id=0, has_side_effects=True, vmem_limit_bytes=52 * 1024 * 1024
        ),
    )(points.reshape(2, blk, width), centroids)
    return newest, previous, row_pot.reshape(rows), list_pot.reshape(lists)


def solution(mesh):
    return jax.shard_map(
        functools.partial(shards, mesh.shape["dp"], mesh.shape["cent"]),
        mesh=mesh,
        in_specs=(P("dp", None), P(("cent", "dp"), None)),
        out_specs=(P(("cent", "dp"), None), P(("cent", "dp"), None), P("dp"), P(("cent", "dp"))),
        check_vma=False,
    )
```

time: 408 us -> 88.2 us (0.22)
  blocking collectives: 162 us -> 0 us
  waiting for transfers between devices: 122 us -> 0 us
  Pallas kernels: 0 us -> 84.5 us
  other arithmetic: 61.8 us -> 0 us
  matrix products: 45.3 us -> 0 us
  between operations: 14.6 us -> 0.64 us
    pallas_call x0 -> x1, Pallas kernels: none -> 84.5 us  [shards(): pl.pallas_call(functools.partial(kernel, n_dp, n_cent), out_shape=(jax.Sh...]
    reduce_scatter x3 -> x0, waiting for transfers between devices: 72.4 us -> none  [shards(): lax.psum_scatter(weighted, 'dp', scatter_dimension=0, tiled=True)]
    pmax x6 -> x0, blocking collectives: 70.9 us -> none  [the longest x3 43.6 us: row_lse(): top = lax.pmax(jnp.max(values, axis=1), 'cent')]
    psum x5 -> x0, blocking collectives: 59.4 us -> none  [the longest x3 41.1 us: row_lse(): total = lax.psum(jnp.sum(jnp.exp(values - top[:, None]), axis=1), 'cent')]
    all_gather x2 -> x0, waiting for transfers between devices: 48.6 us -> none  [shards(): lax.all_gather(used, 'dp', axis=0, tiled=True)]
    dot_general x5 -> x0, matrix products: 45.3 us -> none  [the longest x3 30.2 us: plan_sums(): lax.dot_general(plan.astype(jnp.bfloat16), rows_data, (((0,), (0,)), ((),...]
    reduce_sum x8 -> x0, other arithmetic: 36.8 us -> none  [the longest x3 14.6 us: column_lse(): total = lax.psum(jnp.sum(jnp.exp(values - top[None, :]), axis=0), 'dp')]
    unnamed x2 -> x0, blocking collectives: 32.1 us -> none
  transfers between devices with their start and end apart: 5 -> 0, of which waited for: 3 -> 0; matrix products, arithmetic and copies ran while one was open for 18% -> 0% of each run, Pallas kernels for 0% -> 0%
where the time goes in v1:
time: 88.2 us; the launch traced here: 88 us
  Pallas kernels  84.5 us (96%)
  local copies, waits for them, and re-layouts  2.93 us (3%)
    pallas_call x1, Pallas kernels, shards(): pl.pallas_call(functools.partial(kernel, n_dp, n_cent), out_shape=(jax.Sh...  84.5 us
    unnamed x4, local copies, waits for them, and re-layouts  2.93 us

profile of v1, /device:TPU:0, one launch (start us, length us, event | category | flops | bytes accessed | tf_op | source)
XLA Modules:
  0.0 88.0 jit_solution(9042329517846637102)
XLA Ops:
  0.6 84.5 %shard_map.57 = (bf16[512,768]{1,0:T(8,128)(2,1)S(1)}, bf16[512,768]{1,0:T(8,128)(2,1)S(1)}, f32[2,1,512]{2,1,0:T(1,128)S(1)}, f32[1,512]{1,0:T(1,128)S(1)}) custom-call(bf16[2,512,768]{2,1,0:T(8,128)(2,1)} %bitcast.5, bf16[512,768]{1,0:T(8,128)(2,1)} %cen.1), custom_call_target="tpu_custom_call" | custom-call | tf_op jit(solution)/shard_map/pallas_call | solution.py:369
  85.1 0.9 %copy.10 = bf16[512,768]{1,0:T(8,128)(2,1)} copy(bf16[512,768]{1,0:T(8,128)(2,1)S(1)} %get-tuple-element.16) | data formatting | bytes 1572864
  86.0 0.9 copy.11
  86.9 0.6 copy.12
  87.4 0.6 copy.13

commit v2 on v1

--- a/solution.py
+++ b/solution.py
@@ -62,6 +62,8 @@
     sib = flip(k, 1)
     me = k * n_dp + d
     my_w = lax.rem(me, w_all)
+    w_half = w_all // 2
+    my_half = my_w // w_half
 
     def dev(e):
         return {"dp": lax.rem(e, n_dp), "cent": e // n_dp}
@@ -125,53 +127,93 @@
         return cp_
 
     pending = []
-    if n_dp == 4:
+    if n_dp == 4 and n_cent % 4 == 0:
         dx, dy = flip(d, 1), flip(d, 2)
         dd = flip(dx, 2)
-        part = (pl.ds(0, quarter), pl.ds(quarter, quarter))
         hx, hy, hd, ho = 2 * dx + core, 2 * dy + core, 2 * dd + core, 2 * d + core
         to_x, to_y = {"dp": dx, "cent": k}, {"dp": dy, "cent": k}
-
-        def own_send(slot, p, to):
-            c = remote(pts_in.at[core, part[p]], pts.at[ho, part[p]], ag_send.at[slot], ag_recv.at[slot], to)
+        to_z = {"dp": d, "cent": flip(k, 2)}
+        unit = blk // 4
+        odd = lax.rem(k // 2, 2)
+        first = pl.ds(pl.multiple_of(odd * 3 * unit, unit), unit)
+        other = pl.ds(pl.multiple_of((1 - odd) * 3 * unit, unit), unit)
+        q1, q2 = pl.ds(unit, unit), pl.ds(2 * unit, unit)
+        q2a, q2b = pl.ds(2 * unit, unit // 2), pl.ds(2 * unit + unit // 2, unit // 2)
+
+        def own_send(slot, rows, to):
+            c = remote(pts_in.at[core, rows], pts.at[ho, rows], ag_send.at[slot], ag_recv.at[slot], to)
             c.start()
+            pending.append(c)
             return c
 
-        def relay(slot, j, p, to):
-            ref = pts.at[j, part[p]]
+        def relay(slot, j, rows, to):
+            ref = pts.at[j, rows]
             c = remote(ref, ref, ag_send.at[slot], ag_recv.at[slot], to)
             c.start()
+            pending.append(c)
             return c
 
-        s0 = own_send(0, 1, to_x)
-        s3 = own_send(3, 0, to_y)
-        s1 = own_send(1, 0, to_x)
-        s4 = own_send(4, 1, to_y)
+        shared = {}
+
+        def share(name, j, rows):
+            c = forward(len(shared), j, rows)
+            shared[name] = c
+            pending.append(c)
+
+        x_f = own_send(0, first, to_x)
+        y_f = own_send(1, first, to_y)
+        x_1 = own_send(2, q1, to_x)
+        y_2 = own_send(3, q2, to_y)
+        y_1 = own_send(4, q1, to_y)
         own_copy.wait()
         many_scores([2 * d, 2 * d + 1])
-        s3.wait_recv()
-        s2 = relay(2, hy, 0, to_x)
-        f0 = forward(0, hy, part[0])
-        s0.wait_recv()
-        s5 = relay(5, hx, 1, to_y)
-        f1 = forward(1, hx, part[1])
-        s1.wait_recv()
-        f2 = forward(2, hx, part[0])
-        s4.wait_recv()
-        f3 = forward(3, hy, part[1])
-        many_scores([hx, hy])
-        for f in (f0, f1, f2, f3):
-            f.wait_recv()
-        many_scores([flip(hx, 1), flip(hy, 1)])
-        s2.wait_recv()
-        f4 = forward(4, hd, part[0])
-        s5.wait_recv()
-        f5 = forward(5, hd, part[1])
+        y_f.wait_recv()
+        x_rf = relay(5, hy, first, to_x)
+        x_2b = own_send(6, q2b, to_x)
+        x_2a = own_send(7, q2a, to_x)
+        z_y = relay(8, hy, first, to_z)
+        share("yf", hy, first)
+        x_f.wait_recv()
+        z_x = relay(9, hx, first, to_z)
+        share("xf", hx, first)
+        x_1.wait_recv()
+        y_r1 = relay(10, hx, q1, to_y)
+        share("x1", hx, q1)
+        y_2.wait_recv()
+        x_r2 = relay(11, hy, q2a, to_x)
+        share("y2", hy, q2)
+        z_y.wait_recv()
+        share("yo", hy, other)
+        x_rf.wait_recv()
+        z_d = relay(12, hd, first, to_z)
+        share("df", hd, first)
+        y_1.wait_recv()
+        share("y1", hy, q1)
+        x_2b.wait_recv()
+        y_r2 = relay(13, hx, q2b, to_y)
+        many_scores([hy])
+        z_x.wait_recv()
+        share("xo", hx, other)
+        x_2a.wait_recv()
+        share("x2", hx, q2)
+        for name in ("yf", "y2", "yo", "y1"):
+            shared[name].wait_recv()
+        many_scores([flip(hy, 1), hx])
+        y_r1.wait_recv()
+        share("d1", hd, q1)
+        for name in ("xf", "x1", "xo", "x2"):
+            shared[name].wait_recv()
+        many_scores([flip(hx, 1)])
+        x_r2.wait_recv()
+        share("da", hd, q2a)
+        y_r2.wait_recv()
+        share("db", hd, q2b)
+        z_d.wait_recv()
+        share("do", hd, other)
         many_scores([hd])
-        f4.wait_recv()
-        f5.wait_recv()
+        for name in ("df", "d1", "da", "db", "do"):
+            shared[name].wait_recv()
         many_scores([flip(hd, 1)])
-        pending = [s0, s1, s2, s3, s4, s5, f0, f1, f2, f3, f4, f5]
     else:
         sends = []
         for o in range(1, n_dp):
@@ -206,7 +248,16 @@
 
     def put_chunks(x, i, v):
         for g in range(per):
-            mine[x, i * per + g] = v[:, g * LANES : (g + 1) * LANES]
+            w = i * per + g
+            mine[x, w] = v[:, g * LANES : (g + 1) * LANES]
+            for group in range(n // w_all):
+                owner = group * w_all + w
+
+                @pl.when(owner != me)
+                def _():
+                    remote(
+                        mine.at[x, w], gathered.at[x, me], x1_send.at[x], x1_recv.at[x], dev(owner)
+                    ).start()
 
     def row_pass(ref, x):
         def body(i, _):
@@ -228,23 +279,13 @@
 
         lax.fori_loop(0, nb, body, 0)
 
-    def start_exchange(x):
-        def send(o, _):
-            e = lax.rem(me + o, n)
-            remote(
-                mine.at[x, lax.rem(e, w_all)], gathered.at[x, me], x1_send.at[x], x1_recv.at[x], dev(e)
-            ).start()
-            return 0
-
-        lax.fori_loop(1, n, send, 0)
-        gathered[x, me] = mine[x, my_w]
-
     def wait_bytes(ref, sem):
         pltpu.make_async_copy(ref, ref, sem).wait()
 
     def middle_exchange(x, logs):
         wait_bytes(gathered.at[x, pl.ds(0, n - 1)], x1_recv.at[x])
         wait_bytes(gathered.at[x, pl.ds(0, n - 1)], x1_send.at[x])
+        gathered[x, me] = mine[x, my_w]
         v = gathered[x]
         if logs:
             m = jnp.max(v, axis=0, keepdims=True)
@@ -256,19 +297,27 @@
         def send(o, _):
             e = (me // w_all) * w_all + lax.rem(my_w + o, w_all)
             ref = full.at[x, my_w]
-            remote(ref, ref, x2_send.at[x], x2_recv.at[x], dev(e)).start()
+            remote(ref, ref, x2_send.at[x], x2_recv.at[2 * x + my_half], dev(e)).start()
             return 0
 
         lax.fori_loop(1, w_all, send, 0)
 
-    def end_exchange(x):
-        wait_bytes(full.at[x, pl.ds(0, w_all - 1)], x2_recv.at[x])
-        wait_bytes(full.at[x, pl.ds(0, w_all - 1)], x2_send.at[x])
+    def end_exchange(x, half):
+        @pl.when(my_half == half)
+        def _():
+            wait_bytes(full.at[x, pl.ds(0, w_half - 1)], x2_recv.at[2 * x + half])
+
+        @pl.when(my_half != half)
+        def _():
+            wait_bytes(full.at[x, pl.ds(0, w_half)], x2_recv.at[2 * x + half])
+
+        if half:
+            wait_bytes(full.at[x, pl.ds(0, w_all - 1)], x2_send.at[x])
 
     def full_row(x, i):
         return jnp.concatenate([full[x, i * per + g] for g in range(per)], axis=1)
 
-    def weigh(ref, scale_of):
+    def weigh(ref, scale_of, x=None):
         mass[...] = jnp.zeros_like(mass)
         acc[...] = jnp.zeros_like(acc)
 
@@ -281,7 +330,10 @@
             acc[...] += jnp.dot(pb[...], pts[i], preferred_element_type=jnp.float32)
             return 0
 
-        lax.fori_loop(0, nb, body, 0)
+        for h in range(2):
+            if x is not None:
+                end_exchange(x, h)
+            lax.fori_loop(h * nb // 2, (h + 1) * nb // 2, body, 0)
 
     def refresh(out, used, gain):
         for s in strips:
@@ -295,16 +347,14 @@
 
     finish_columns()
     row_pass(lt, 0)
-    start_exchange(0)
     middle_exchange(0, True)
-    end_exchange(0)
 
     def scale_0(i):
         v = jnp.exp2(row_m[i] - full_row(0, i))
         row_a[i] = v
         return v
 
-    weigh(lt, scale_0)
+    weigh(lt, scale_0, 0)
     refresh(c1, cen, False)
     for s in strips:
         m = jnp.sum(mass[s, :], axis=1, keepdims=True)
@@ -319,7 +369,6 @@
         return 0
 
     lax.fori_loop(0, nb, row_sums, 0)
-    start_exchange(1)
 
     def second_scores(i, _):
         dot_scores(c1, i, lt2)
@@ -328,7 +377,6 @@
     lax.fori_loop(0, nb // 2, second_scores, 0)
     middle_exchange(1, False)
     lax.fori_loop(nb // 2, nb, second_scores, 0)
-    end_exchange(1)
 
     top[...] = jnp.full_like(top, -jnp.inf)
     tot[...] = jnp.zeros_like(tot)
@@ -341,15 +389,15 @@
             online(lt2[i, s, :] + pot, s)
         return 0
 
-    lax.fori_loop(0, nb, second_columns, 0)
+    for h in range(2):
+        end_exchange(1, h)
+        lax.fori_loop(h * nb // 2, (h + 1) * nb // 2, second_columns, 0)
     finish_columns()
     row_pass(lt2, 2)
-    start_exchange(2)
     middle_exchange(2, True)
     weigh(lt, lambda i: row_b[i])
     refresh(previous, cen, True)
-    end_exchange(2)
-    weigh(lt2, lambda i: jnp.exp2(row_m[i] - full_row(2, i)))
+    weigh(lt2, lambda i: jnp.exp2(row_m[i] - full_row(2, i)), 2)
     refresh(newest, c1, False)
     for h in range(2):
         row_out[h] = -LN2 * full_row(2, 2 * d + h)
@@ -394,8 +442,8 @@
             pltpu.VMEM((3, w_all, 1, LANES), f32),
             pltpu.VMEM((3, n, 1, LANES), f32),
             pltpu.VMEM((3, w_all, 1, LANES), f32),
-            dma, dma((2 * n_dp,)), dma((2 * n_dp,)), dma((2 * n_dp,)), dma((2 * n_dp,)),
-            dma((3,)), dma((3,)), dma((3,)), dma((3,)),
+            dma, dma((14,)), dma((14,)), dma((13,)), dma((13,)),
+            dma((3,)), dma((3,)), dma((3,)), dma((6,)),
         ],
         compiler_params=pltpu.CompilerParams(
             collective_id=0, has_side_effects=True, vmem_limit_bytes=52 * 1024 * 1024

time: 88.2 us -> 76.6 us (0.87)
  Pallas kernels: 84.5 us -> 72.9 us
    pallas_call x1, Pallas kernels: 84.5 us -> 72.9 us  [shards(): pl.pallas_call(functools.partial(kernel, n_dp, n_cent), out_shape=(jax.Sh...]
where the time goes in v2:
time: 76.6 us; the launch traced here: 76.5 us
  Pallas kernels  72.9 us (95%)
  local copies, waits for them, and re-layouts  2.93 us (4%)
    pallas_call x1, Pallas kernels, shards(): pl.pallas_call(functools.partial(kernel, n_dp, n_cent), out_shape=(jax.Sh...  72.9 us
    unnamed x4, local copies, waits for them, and re-layouts  2.93 us

profile of v2, /device:TPU:0, one launch (start us, length us, event | category | flops | bytes accessed | tf_op | source)
XLA Modules:
  0.0 76.5 jit_solution(6314720930002980978)
XLA Ops:
  0.6 72.9 %shard_map.57 = (bf16[512,768]{1,0:T(8,128)(2,1)S(1)}, bf16[512,768]{1,0:T(8,128)(2,1)S(1)}, f32[2,1,512]{2,1,0:T(1,128)S(1)}, f32[1,512]{1,0:T(1,128)S(1)}) custom-call(bf16[2,512,768]{2,1,0:T(8,128)(2,1)} %bitcast.5, bf16[512,768]{1,0:T(8,128)(2,1)} %cen.1), custom_call_target="tpu_custom_call" | custom-call | tf_op jit(solution)/shard_map/pallas_call | solution.py:417
  73.5 0.9 %copy.10 = bf16[512,768]{1,0:T(8,128)(2,1)} copy(bf16[512,768]{1,0:T(8,128)(2,1)S(1)} %get-tuple-element.16) | data formatting | bytes 1572864
  74.4 0.9 %copy.11 = bf16[512,768]{1,0:T(8,128)(2,1)} copy(bf16[512,768]{1,0:T(8,128)(2,1)S(1)} %get-tuple-element.17) | data formatting | bytes 1572864
  75.3 0.6 copy.12
  75.9 0.6 copy.13

commit v3 on v2

--- a/solution.py
+++ b/solution.py
@@ -38,7 +38,7 @@
     n_dp, n_cent,
     pts_in, cen,
     newest, previous, row_out, list_out,
-    pts, lt, lt2, pb, acc, c1, top, tot, cp, ratio_j, mass, row_a, row_b, row_m,
+    pts, lt, lt2, pb, pb2, acc, c1, top, tot, cp, ratio_j, mass, row_a, row_b, row_m,
     mine, gathered, full,
     own_sem, ag_send, ag_recv, sib_send, sib_recv, x1_send, x1_recv, x2_send, x2_recv,
 ):
@@ -321,19 +321,35 @@
         mass[...] = jnp.zeros_like(mass)
         acc[...] = jnp.zeros_like(acc)
 
-        def body(i, _):
+        def fill(to, i):
             scale = scale_of(i)
             for s in strips:
                 p = ref[i, s, :] * scale
                 mass[s, :] += fold(jnp.add, lane_groups(p))
-                pb[s, :] = p.astype(jnp.bfloat16)
-            acc[...] += jnp.dot(pb[...], pts[i], preferred_element_type=jnp.float32)
+                to[s, :] = p.astype(jnp.bfloat16)
+
+        slots = (pb, pb2)
+        steps = 4
+        groups = nb // steps
+
+        def body(t, _):
+            if x is not None:
+                for h in range(2):
+
+                    @pl.when(t == h * (groups // 2))
+                    def _():
+                        end_exchange(x, h)
+
+            fill(slots[0], t * steps)
+            for u in range(steps):
+                if u + 1 < steps:
+                    fill(slots[(u + 1) % 2], t * steps + u + 1)
+                acc[...] += jnp.dot(
+                    slots[u % 2][...], pts[t * steps + u], preferred_element_type=jnp.float32
+                )
             return 0
 
-        for h in range(2):
-            if x is not None:
-                end_exchange(x, h)
-            lax.fori_loop(h * nb // 2, (h + 1) * nb // 2, body, 0)
+        lax.fori_loop(0, groups, body, 0)
 
     def refresh(out, used, gain):
         for s in strips:
@@ -429,6 +445,7 @@
             pltpu.VMEM((nb, lists, blk), f32),
             pltpu.VMEM((nb, lists, blk), f32),
             pltpu.VMEM((lists, blk), bf16),
+            pltpu.VMEM((lists, blk), bf16),
             pltpu.VMEM((lists, width), f32),
             pltpu.VMEM((lists, width), bf16),
             pltpu.VMEM((lists, LANES), f32),

time: 76.6 us -> 74.1 us (0.967)
  Pallas kernels: 72.9 us -> 70.4 us
    pallas_call x1, Pallas kernels: 72.9 us -> 70.4 us  [shards(): pl.pallas_call(functools.partial(kernel, n_dp, n_cent), out_shape=(jax.Sh...]
where the time goes in v3:
time: 74.1 us; the launch traced here: 74 us
  Pallas kernels  70.4 us (95%)
  local copies, waits for them, and re-layouts  2.93 us (4%)
    pallas_call x1, Pallas kernels, shards(): pl.pallas_call(functools.partial(kernel, n_dp, n_cent), out_shape=(jax.Sh...  70.4 us
    unnamed x4, local copies, waits for them, and re-layouts  2.93 us

profile of v3, /device:TPU:0, one launch (start us, length us, event | category | flops | bytes accessed | tf_op | source)
XLA Modules:
  0.0 74.0 jit_solution(11789056587115225018)
XLA Ops:
  0.6 70.4 %shard_map.57 = (bf16[512,768]{1,0:T(8,128)(2,1)S(1)}, bf16[512,768]{1,0:T(8,128)(2,1)S(1)}, f32[2,1,512]{2,1,0:T(1,128)S(1)}, f32[1,512]{1,0:T(1,128)S(1)}) custom-call(bf16[2,512,768]{2,1,0:T(8,128)(2,1)} %bitcast.5, bf16[512,768]{1,0:T(8,128)(2,1)} %cen.1), custom_call_target="tpu_custom_call" | custom-call | tf_op jit(solution)/shard_map/pallas_call | solution.py:433
  71.0 0.9 %copy.10 = bf16[512,768]{1,0:T(8,128)(2,1)} copy(bf16[512,768]{1,0:T(8,128)(2,1)S(1)} %get-tuple-element.16) | data formatting | bytes 1572864
  71.9 0.9 %copy.11 = bf16[512,768]{1,0:T(8,128)(2,1)} copy(bf16[512,768]{1,0:T(8,128)(2,1)S(1)} %get-tuple-element.17) | data formatting | bytes 1572864
  72.8 0.6 copy.12
  73.4 0.6 copy.13

commit v4 on v3

--- a/solution.py
+++ b/solution.py
@@ -40,7 +40,7 @@
     newest, previous, row_out, list_out,
     pts, lt, lt2, pb, pb2, acc, c1, top, tot, cp, ratio_j, mass, row_a, row_b, row_m,
     mine, gathered, full,
-    own_sem, ag_send, ag_recv, sib_send, sib_recv, x1_send, x1_recv, x2_send, x2_recv,
+    own_sem, rounds, ag_send, ag_recv, sib_send, sib_recv, x1_send, x1_recv, x2_send, x2_recv,
 ):
     n = n_dp * n_cent
     _, blk, width = pts_in.shape
@@ -70,17 +70,23 @@
 
     barrier = pltpu.get_barrier_semaphore()
 
-    def greet(o, _):
-        e = lax.rem(me + o, n)
-        pl.semaphore_signal(barrier, inc=1, device_id=dev(e), device_id_type=pl.DeviceIdType.MESH)
-        return 0
-
-    lax.fori_loop(1, n, greet, 0)
+    partners = [{"dp": flip(d, 1 << b), "cent": k} for b in range(n_dp.bit_length() - 1)]
+    partners += [{"dp": d, "cent": flip(k, 1 << b)} for b in range(n_cent.bit_length() - 1)]
+    for to in partners:
+        pl.semaphore_signal(barrier, inc=1, device_id=to, device_id_type=pl.DeviceIdType.MESH)
     own_copy = pltpu.make_async_copy(pts_in, pts.at[pl.ds(2 * d, 2)], own_sem)
     own_copy.start()
     top[...] = jnp.full_like(top, -jnp.inf)
     tot[...] = jnp.zeros_like(tot)
-    pl.semaphore_wait(barrier, n - 1)
+    pl.semaphore_wait(barrier, len(partners))
+
+    def tell(r):
+        pl.semaphore_signal(
+            rounds.at[r], inc=1, device_id=partners[r], device_id_type=pl.DeviceIdType.MESH
+        )
+
+    def hear(r):
+        pl.semaphore_wait(rounds.at[r], 1)
 
     def remote(src, dst, ss, rs, to):
         return pltpu.make_async_remote_copy(
@@ -127,7 +133,7 @@
         return cp_
 
     pending = []
-    if n_dp == 4 and n_cent % 4 == 0:
+    if n_dp == 4 and n_cent == 8:
         dx, dy = flip(d, 1), flip(d, 2)
         dd = flip(dx, 2)
         hx, hy, hd, ho = 2 * dx + core, 2 * dy + core, 2 * dd + core, 2 * d + core
@@ -165,8 +171,11 @@
         x_1 = own_send(2, q1, to_x)
         y_2 = own_send(3, q2, to_y)
         y_1 = own_send(4, q1, to_y)
+        tell(0)
         own_copy.wait()
         many_scores([2 * d, 2 * d + 1])
+        hear(0)
+        tell(1)
         y_f.wait_recv()
         x_rf = relay(5, hy, first, to_x)
         x_2b = own_send(6, q2b, to_x)
@@ -176,12 +185,16 @@
         x_f.wait_recv()
         z_x = relay(9, hx, first, to_z)
         share("xf", hx, first)
+        hear(1)
+        tell(2)
         x_1.wait_recv()
         y_r1 = relay(10, hx, q1, to_y)
         share("x1", hx, q1)
         y_2.wait_recv()
         x_r2 = relay(11, hy, q2a, to_x)
         share("y2", hy, q2)
+        hear(2)
+        tell(3)
         z_y.wait_recv()
         share("yo", hy, other)
         x_rf.wait_recv()
@@ -189,9 +202,12 @@
         share("df", hd, first)
         y_1.wait_recv()
         share("y1", hy, q1)
+        hear(3)
+        tell(4)
         x_2b.wait_recv()
         y_r2 = relay(13, hx, q2b, to_y)
         many_scores([hy])
+        hear(4)
         z_x.wait_recv()
         share("xo", hx, other)
         x_2a.wait_recv()
@@ -215,6 +231,9 @@
             shared[name].wait_recv()
         many_scores([flip(hd, 1)])
     else:
+        for r in range(len(partners)):
+            tell(r)
+            hear(r)
         sends = []
         for o in range(1, n_dp):
             c = remote(
@@ -294,13 +313,25 @@
             res = jnp.sum(v, axis=0, keepdims=True)
         full[x, my_w] = res[0]
 
-        def send(o, _):
-            e = (me // w_all) * w_all + lax.rem(my_w + o, w_all)
-            ref = full.at[x, my_w]
-            remote(ref, ref, x2_send.at[x], x2_recv.at[2 * x + my_half], dev(e)).start()
-            return 0
-
-        lax.fori_loop(1, w_all, send, 0)
+        ref = full.at[x, my_w]
+
+        def send_to(to):
+            remote(ref, ref, x2_send.at[x], x2_recv.at[2 * x + my_half], to).start()
+
+        if n == w_all:
+            cents = [lax.rem(k + o, n_cent) for o in range(n_cent)]
+            dps = [lax.rem(d + o, n_dp) for o in range(n_dp)]
+            for oc in sorted(range(n_cent), key=lambda o: abs(2 * o - n_cent)):
+                for od in range(n_dp):
+                    if oc or od:
+                        send_to({"dp": dps[od], "cent": cents[oc]})
+        else:
+
+            def send(o, _):
+                send_to(dev((me // w_all) * w_all + lax.rem(my_w + o, w_all)))
+                return 0
+
+            lax.fori_loop(1, w_all, send, 0)
 
     def end_exchange(x, half):
         @pl.when(my_half == half)
@@ -459,7 +490,7 @@
             pltpu.VMEM((3, w_all, 1, LANES), f32),
             pltpu.VMEM((3, n, 1, LANES), f32),
             pltpu.VMEM((3, w_all, 1, LANES), f32),
-            dma, dma((14,)), dma((14,)), dma((13,)), dma((13,)),
+            dma, pltpu.SemaphoreType.REGULAR((16,)), dma((14,)), dma((14,)), dma((13,)), dma((13,)),
             dma((3,)), dma((3,)), dma((3,)), dma((6,)),
         ],
         compiler_params=pltpu.CompilerParams(

time: 74.1 us -> 72.2 us (0.974)
  Pallas kernels: 70.4 us -> 68.5 us
    pallas_call x1, Pallas kernels: 70.4 us -> 68.5 us  [shards(): pl.pallas_call(functools.partial(kernel, n_dp, n_cent), out_shape=(jax.Sh...]
where the time goes in v4:
time: 72.2 us; the launch traced here: 72.1 us
  Pallas kernels  68.5 us (95%)
  local copies, waits for them, and re-layouts  2.93 us (4%)
    pallas_call x1, Pallas kernels, shards(): pl.pallas_call(functools.partial(kernel, n_dp, n_cent), out_shape=(jax.Sh...  68.5 us
    unnamed x4, local copies, waits for them, and re-layouts  2.93 us

profile of v4, /device:TPU:0, one launch (start us, length us, event | category | flops | bytes accessed | tf_op | source)
XLA Modules:
  0.0 72.1 jit_solution(5367584867931865885)
XLA Ops:
  0.6 68.5 %shard_map.57 = (bf16[512,768]{1,0:T(8,128)(2,1)S(1)}, bf16[512,768]{1,0:T(8,128)(2,1)S(1)}, f32[2,1,512]{2,1,0:T(1,128)S(1)}, f32[1,512]{1,0:T(1,128)S(1)}) custom-call(bf16[2,512,768]{2,1,0:T(8,128)(2,1)} %bitcast.5, bf16[512,768]{1,0:T(8,128)(2,1)} %cen.1), custom_call_target="tpu_custom_call" | custom-call | tf_op jit(solution)/shard_map/pallas_call | solution.py:464
  69.1 0.9 %copy.10 = bf16[512,768]{1,0:T(8,128)(2,1)} copy(bf16[512,768]{1,0:T(8,128)(2,1)S(1)} %get-tuple-element.16) | data formatting | bytes 1572864
  70.0 0.9 %copy.11 = bf16[512,768]{1,0:T(8,128)(2,1)} copy(bf16[512,768]{1,0:T(8,128)(2,1)S(1)} %get-tuple-element.17) | data formatting | bytes 1572864
  70.9 0.6 copy.12
  71.5 0.6 copy.13
